TPU v7x, 256 devices: a whole 4x4x8 slice. The times are simulated.
256 devices in a mesh: sec: 16 (over z, core), op: 16 (over x, y).
Axes of the slice: x: 4, y: 4, z: 8, core: 2. Of those that a mesh axis runs over, the one named last changes fastest.
Arguments:
- theta: float32 [32, 512, 512], P('sec', 'op'), may hold values from -6 to 6
- counts: int32 [32], P('sec'), may hold values from 256 to 512, as said below
- pair_source: int32 [256], P('sec'), may hold values from 0 to 1
- pair_target: int32 [256], P('sec'), may hold values from 0 to 31
- left_ops: float32 [1024, 512, 512], P(('sec', 'op')), may hold values from -0.25 to 0.25
- right_ops: float32 [1024, 512, 512], P(('sec', 'op')), may hold values from -0.25 to 0.25
Outputs:
- cheb_last: float32 [32, 512, 512], P('sec', 'op')
- cheb_prev: float32 [32, 512, 512], P('sec', 'op')
Inputs may be any that keep to these rules, and one draw needn't show every extreme that they name: `counts`: every sector has between 256 and 512 live states; some sector has exactly 512 and some exactly 256.
All inputs are finite; a program needn't handle non-finite values.
Results may differ from a plain program's by a relative error of at most 0.0001.
Values sent between devices are 32-bit elements; how exact they have to be, the bound alone decides.
A program may use at most 64 MiB of HBM per device.

v0:
```python
import math

import jax
import jax.numpy as jnp
from jax import lax
from jax.sharding import PartitionSpec as P

STEPS = 3


def per_device(theta, counts, pair_source, pair_target, left_ops, right_ops):
    op_count = lax.axis_size("op")
    op_place = lax.axis_index("op")
    sec_place = lax.axis_index("sec")
    sec_local = theta.shape[0]
    row_count = theta.shape[1]
    order_size = theta.shape[2]
    pairs_local = left_ops.shape[0]
    group_blocks = pair_target.shape[0]
    sectors_all = sec_local * lax.axis_size("sec")
    factor = 0.5 / math.sqrt(group_blocks * pairs_local / sec_local)
    highest = lax.Precision.HIGHEST
    my_source = lax.dynamic_index_in_dim(pair_source, op_place, 0, keepdims=False)
    row_numbers = op_place * row_count + jnp.arange(row_count, dtype=jnp.int32)
    row_alive = row_numbers[None, :] < counts[:, None]
    column_alive = jnp.arange(order_size, dtype=jnp.int32)[None, :] < counts[:, None]
    live_mask = (row_alive[:, :, None] & column_alive[:, None, :]).astype(jnp.float32)
    target_hot = (pair_target[None, :] == jnp.arange(sectors_all, dtype=jnp.int32)[:, None]).astype(
        jnp.float32
    )

    def hamiltonian(iterate):
        gathered = lax.all_gather(iterate, "op", axis=1, tiled=True)
        chosen = lax.dynamic_index_in_dim(gathered, my_source, 0, keepdims=False)
        left_product = jnp.einsum("pmr,rn->pmn", left_ops, chosen, precision=highest)
        block_term = jnp.einsum("pmk,pnk->mn", left_product, right_ops, precision=highest)
        split_rows = block_term.reshape(op_count, row_count, order_size)
        block_rows = lax.all_to_all(split_rows, "op", split_axis=0, concat_axis=0, tiled=True)
        flat_rows = block_rows.reshape(group_blocks, row_count * order_size)
        sector_sums = jnp.dot(
            target_hot, flat_rows, precision=highest, preferred_element_type=jnp.float32
        )
        sector_sums = sector_sums.reshape(sectors_all, row_count, order_size)
        whole_sums = lax.psum(sector_sums, "sec")
        own_sums = lax.dynamic_slice_in_dim(whole_sums, sec_place * sec_local, sec_local, 0)
        return factor * own_sums * live_mask

    previous = theta * live_mask
    current = hamiltonian(previous)
    for step_number in range(STEPS - 1):
        following = 2.0 * hamiltonian(current) - previous
        previous, current = (current, following)
    return (current, previous)


def solution(mesh):
    in_specs = (
        P("sec", "op", None),
        P("sec"),
        P("sec"),
        P("sec"),
        P(("sec", "op"), None, None),
        P(("sec", "op"), None, None),
    )
    out_specs = (P("sec", "op", None), P("sec", "op", None))
    return jax.shard_map(
        per_device, mesh=mesh, in_specs=in_specs, out_specs=out_specs, check_vma=False
    )
```

profile of v0, /device:TPU:1, one launch (start us, length us, event | category | flops | bytes accessed | tf_op | source)
XLA Modules:
  0.0 675.0 jit_solution(8471230393268469698)
XLA Ops:
  7.2 0.0 all-gather.4.cloned.1.call-start
  7.2 0.7 iota_compare_fusion.1
  8.0 0.7 broadcast_compare_fusion
  8.7 1.7 and_select_fusion.3
  10.4 0.0 all-gather.4.cloned.1.call-update
  10.4 0.0 all-reduce.4.cloned.1.call-start
  10.5 1.2 dynamic_slice.23
  13.7 50.3 %all-gather.4.cloned.1.call-done = f32[2,512,512]{2,0,1:T(2,128)} async-done(((f32[2,32,512]{2,0,1:T(2,128)}), f32[2,512,512]{2,0,1:T(2,128)}) %all-gather.4.cloned.1.call-update) | async-done | bytes 2097168 | tf_op jit(solution)/shard_map/all_gather | solution.py:33
  63.9 2.5 constant_dynamic-slice_fusion.2
  66.4 1.3 copy.18
  67.8 0.0 copy-start
  67.8 10.3 %fusion.19 = f32[512,4,512]{2,0,1:T(8,128)S(1)} fusion(f32[4,512,512]{2,1,0:T(8,128)} %param.10, f32[1,512,512]{1,2,0:T(8,128)S(1)} %copy.18), kind=kOutput, calls=%fused_computation.19 | convolution fusion | flops 6442450944 | bytes 9437184 | tf_op jit(solution)/shard_map/pmr,rn->pmn/dot_general | solution.py:35
  78.1 0.0 copy-done
  78.1 0.0 copy-start.5
  78.1 13.9 %fusion.4 = f32[512,512,1]{1,0,2:T(8,128)S(1)} fusion(f32[4,512,512]{2,1,0:T(8,128)S(1)} %copy-done, f32[512,4,512]{2,0,1:T(8,128)S(1)} %fusion.19), kind=kOutput, calls=%fused_computation.4 | convolution fusion | flops 6442450944 | bytes 9437184 | tf_op jit(solution)/shard_map/pmk,pnk->mn/dot_general | solution.py:36
  92.0 19.3 %all_to_all.15 = f32[16,32,512]{2,1,0:T(8,128)S(1)} all-to-all(f32[16,32,512]{2,1,0:T(8,128)S(1)} %bitcast.75), channel_id=1, replica_groups=mesh['sec'=16,'op'=16] {'op'}, dimensions={0} | all-to-all | bytes 2097152 | tf_op jit(solution)/shard_map/all_to_all | solution.py:38
  111.3 0.0 copy-done.5
  111.3 2.9 fusion.12
  114.2 0.0 all-reduce.4.cloned.1.call-update
  114.2 0.0 all-gather.6.cloned.1.call-start
  114.2 115.1 %all-reduce.4.cloned.1.call-done = f32[32,32,512]{2,0,1:T(8,128)} async-done(((f32[32,32,512]{2,0,1:T(8,128)}), f32[32,32,512]{2,0,1:T(8,128)}) %all-reduce.4.cloned.1.call-update) | async-done | bytes 2097168 | tf_op jit(solution)/shard_map/psum | solution.py:44
  229.4 1.8 and_select_fusion.2
  231.2 0.0 all-gather.6.cloned.1.call-update
  231.3 0.0 all-reduce.6.cloned.1.call-start
  231.3 50.7 %all-gather.6.cloned.1.call-done = f32[2,512,512]{2,0,1:T(2,128)} async-done(((f32[2,32,512]{2,0,1:T(2,128)}), f32[2,512,512]{2,0,1:T(2,128)}) %all-gather.6.cloned.1.call-update) | async-done | bytes 2097168 | tf_op jit(solution)/shard_map/all_gather | solution.py:33
  282.0 2.5 constant_dynamic-slice_fusion.1
  284.5 1.3 copy.21
  285.8 0.0 copy-start.1
  285.8 10.3 %fusion.17 = f32[512,4,512]{2,0,1:T(8,128)S(1)} fusion(f32[4,512,512]{2,1,0:T(8,128)} %param.10, f32[1,512,512]{1,2,0:T(8,128)S(1)} %copy.21), kind=kOutput, calls=%fused_computation.17 | convolution fusion | flops 6442450944 | bytes 9437184 | tf_op jit(solution)/shard_map/pmr,rn->pmn/dot_general | solution.py:35
  296.1 0.0 copy-done.1
  296.1 13.7 %fusion.2 = f32[512,512,1]{1,0,2:T(8,128)S(1)} fusion(f32[4,512,512]{2,1,0:T(8,128)S(1)} %copy-done.1, f32[512,4,512]{2,0,1:T(8,128)S(1)} %fusion.17), kind=kOutput, calls=%fused_computation.2 | convolution fusion | flops 6442450944 | bytes 9437184 | tf_op jit(solution)/shard_map/pmk,pnk->mn/dot_general | solution.py:36
  309.8 0.0 copy-start.4
  309.9 19.4 %all_to_all.16 = f32[16,32,512]{2,1,0:T(8,128)S(1)} all-to-all(f32[16,32,512]{2,1,0:T(8,128)S(1)} %bitcast.76), channel_id=1, replica_groups=mesh['sec'=16,'op'=16] {'op'}, dimensions={0} | all-to-all | bytes 2097152 | tf_op jit(solution)/shard_map/all_to_all | solution.py:38
  329.2 2.9 fusion.9
  332.1 0.0 all-reduce.6.cloned.1.call-update
  332.2 0.0 all-gather.8.cloned.1.call-start
  332.2 115.3 %all-reduce.6.cloned.1.call-done = f32[32,32,512]{2,0,1:T(8,128)} async-done(((f32[32,32,512]{2,0,1:T(8,128)}), f32[32,32,512]{2,0,1:T(8,128)}) %all-reduce.6.cloned.1.call-update) | async-done | bytes 2097168 | tf_op jit(solution)/shard_map/psum | solution.py:44
  447.5 0.0 copy-done.4
  447.5 1.9 fusion.22
  449.5 0.0 all-gather.8.cloned.1.call-update
  449.5 0.0 all-reduce.8.cloned.1.call-start
  449.5 50.4 %all-gather.8.cloned.1.call-done = f32[2,512,512]{2,0,1:T(2,128)} async-done(((f32[2,32,512]{2,0,1:T(2,128)}), f32[2,512,512]{2,0,1:T(2,128)}) %all-gather.8.cloned.1.call-update) | async-done | bytes 2097168 | tf_op jit(solution)/shard_map/all_gather | solution.py:33
  500.0 2.5 constant_dynamic-slice_fusion
  502.5 1.3 copy.24
  503.8 0.0 copy-start.2
  503.8 10.3 %fusion.15 = f32[512,4,512]{2,0,1:T(8,128)S(1)} fusion(f32[4,512,512]{2,1,0:T(8,128)} %param.10, f32[1,512,512]{1,2,0:T(8,128)S(1)} %copy.24), kind=kOutput, calls=%fused_computation.15 | convolution fusion | flops 6442450944 | bytes 9437184 | tf_op jit(solution)/shard_map/pmr,rn->pmn/dot_general | solution.py:35
  514.1 0.0 copy-done.2
  514.1 13.8 %fusion = f32[512,512,1]{1,0,2:T(8,128)S(1)} fusion(f32[4,512,512]{2,1,0:T(8,128)S(1)} %copy-done.2, f32[512,4,512]{2,0,1:T(8,128)S(1)} %fusion.15), kind=kOutput, calls=%fused_computation | convolution fusion | flops 6442450944 | bytes 9437184 | tf_op jit(solution)/shard_map/pmk,pnk->mn/dot_general | solution.py:36
  528.0 0.0 copy-start.3
  528.0 19.4 %all_to_all.17 = f32[16,32,512]{2,1,0:T(8,128)S(1)} all-to-all(f32[16,32,512]{2,1,0:T(8,128)S(1)} %bitcast.77), channel_id=1, replica_groups=mesh['sec'=16,'op'=16] {'op'}, dimensions={0} | all-to-all | bytes 2097152 | tf_op jit(solution)/shard_map/all_to_all | solution.py:38
  547.4 2.9 fusion.6
  550.3 0.0 all-reduce.8.cloned.1.call-update
  550.3 0.0 copy-done.3
  550.3 0.7 copy.28
  551.0 114.5 %all-reduce.8.cloned.1.call-done = f32[32,32,512]{2,0,1:T(8,128)} async-done(((f32[32,32,512]{2,0,1:T(8,128)}), f32[32,32,512]{2,0,1:T(8,128)}) %all-reduce.8.cloned.1.call-update) | async-done | bytes 2097168 | tf_op jit(solution)/shard_map/psum | solution.py:44
  665.5 1.4 fusion.24
  666.9 0.7 copy.27
  (1 shorter events, 0.0 us)
Async XLA Ops:
  7.2 56.8 %all-gather.4.cloned.1.call-start = ((), (), s32[]{:S(2)}) async-start(), calls=%async_computation.3 | async-start | bytes 2228224 | tf_op jit(solution)/shard_map/all_gather | solution.py:33
  10.4 219.0 %all-reduce.4.cloned.1.call-start = ((), (), s32[]{:S(2)}) async-start(), calls=%async_computation.4 | async-start | bytes 4194304 | tf_op jit(solution)/shard_map/psum | solution.py:44
  67.8 10.3 %copy-start = (f32[4,512,512]{2,1,0:T(8,128)S(1)}, f32[4,512,512]{2,1,0:T(8,128)}, u32[]{:S(2)}) copy-start(f32[4,512,512]{2,1,0:T(8,128)} %param.11) | copy-start | bytes 12582916
  78.1 33.2 %copy-start.5 = (s32[16]{0:T(128)S(1)}, s32[16]{0:T(128)}, u32[]{:S(2)}) copy-start(s32[16]{0:T(128)} %param.9) | copy-start | bytes 196
  114.2 167.8 %all-gather.6.cloned.1.call-start = ((), (), s32[]{:S(2)}) async-start(), calls=%async_computation.5 | async-start | bytes 2228224 | tf_op jit(solution)/shard_map/all_gather | solution.py:33
  231.3 216.3 %all-reduce.6.cloned.1.call-start = ((), (), s32[]{:S(2)}) async-start(), calls=%async_computation.6 | async-start | bytes 4194304 | tf_op jit(solution)/shard_map/psum | solution.py:44
  285.8 10.3 %copy-start.1 = (f32[4,512,512]{2,1,0:T(8,128)S(1)}, f32[4,512,512]{2,1,0:T(8,128)}, u32[]{:S(2)}) copy-start(f32[4,512,512]{2,1,0:T(8,128)} %param.11) | copy-start | bytes 12582916
  309.8 137.7 %copy-start.4 = (f32[2,32,512]{2,1,0:T(8,128)S(1)}, f32[2,32,512]{2,1,0:T(8,128)}, u32[]{:S(2)}) copy-start(f32[2,32,512]{2,1,0:T(8,128)} %param.6) | copy-start | bytes 393220
  332.2 167.8 %all-gather.8.cloned.1.call-start = ((), (), s32[]{:S(2)}) async-start(), calls=%async_computation.7 | async-start | bytes 2228224 | tf_op jit(solution)/shard_map/all_gather | solution.py:33
  449.5 216.0 %all-reduce.8.cloned.1.call-start = ((), (), s32[]{:S(2)}) async-start(), calls=%async_computation.8 | async-start | bytes 4194304 | tf_op jit(solution)/shard_map/psum | solution.py:44
  503.8 10.4 %copy-start.2 = (f32[4,512,512]{2,1,0:T(8,128)S(1)}, f32[4,512,512]{2,1,0:T(8,128)}, u32[]{:S(2)}) copy-start(f32[4,512,512]{2,1,0:T(8,128)} %param.11) | copy-start | bytes 12582916
  528.0 22.3 %copy-start.3 = (f32[2,32,512]{2,0,1:T(2,128)S(1)}, f32[2,32,512]{2,0,1:T(2,128)}, u32[]{:S(2)}) copy-start(f32[2,32,512]{2,0,1:T(2,128)} %fusion.22) | copy-start | bytes 393220
Sparse Core Ops, SparseCore 0:
  11.0 52.8 all-gather.3
  114.3 115.0 all-reduce.3
  232.4 49.5 all-gather.5
  332.3 115.2 all-reduce.5
  450.4 49.5 all-gather.7
  550.4 115.0 all-reduce.7
where the time goes:
time: 680 us; the launch traced here: 675 us
  waiting for transfers between devices  496 us (73%)
  matrix products  81 us (12%)
  blocking collectives  58 us (9%)
  between operations  16.7 us (2%)
  local copies, waits for them, and re-layouts  14 us (2%)
  other arithmetic  8.39 us (1%)
    psum x3, waiting for transfers between devices, hamiltonian(): whole_sums = lax.psum(sector_sums, 'sec')  345 us
    all_gather x3, waiting for transfers between devices, hamiltonian(): gathered = lax.all_gather(iterate, 'op', axis=1, tiled=True)  151 us
    all_to_all x3, blocking collectives, hamiltonian(): lax.all_to_all(split_rows, 'op', split_axis=0, concat_axis=0, tiled=True)  58 us
    dot_general x3, matrix products, hamiltonian(): jnp.einsum('pmk,pnk->mn', left_product, right_ops, precision=highest)  41.5 us
    dot_general x3, matrix products, hamiltonian(): jnp.einsum('pmr,rn->pmn', left_ops, chosen, precision=highest)  30.9 us
  transfers between devices with their start and end apart: 6, of which 6 were waited for; matrix products, arithmetic and copies ran while one was open for 0% of the time, Pallas kernels for 0%

commit v1 on v0

v1 whole, which is shorter than its diff:
```python
import functools
import math

import jax
import jax.numpy as jnp
from jax import lax
from jax.experimental import pallas as pl
from jax.experimental.pallas import tpu as pltpu
from jax.sharding import PartitionSpec as P

STEPS = 3
CHUNKS = 4
HOPS = 4
MESH = pl.DeviceIdType.MESH
F32 = jnp.float32
BF16 = jnp.bfloat16
NT = (((1,), (1,)), ((), ()))


def split(value):
    high = value.astype(BF16)
    return high, (value - high.astype(F32)).astype(BF16)


def kernel(
    factor,
    theta, counts, source, target, left, right,
    last_out, prev_out,
    left_raw, right_raw, left_hi, left_lo, right_two, x_hi, x_lo,
    current, previous, chosen, gathered, terms, arrived, running,
    pass_out, pass_in, sums, ring_in,
    before, final,
    load_sem, gather_send, gather_recv, rows_send, rows_recv,
    pass_send, pass_recv, ring_send, ring_recv,
):
    sec, op = lax.axis_index("sec"), lax.axis_index("op")
    z, core = sec // 2, sec % 2
    op_x, op_y = op // 4, op % 4
    size = left.shape[1]
    pairs = left.shape[0]
    width = size // CHUNKS
    rows = theta.shape[1]
    blocks = target.shape[0]
    sectors = final.shape[0]

    load_left = pltpu.make_async_copy(left, left_raw, load_sem.at[0])
    load_right = pltpu.make_async_copy(right, right_raw, load_sem.at[1])
    load_left.start()
    load_right.start()

    def op_peer(k):
        return ((op_x + k // 4) % 4) * 4 + (op_y + k % 4) % 4

    barrier = pltpu.get_barrier_semaphore()

    @pl.loop(1, blocks)
    def _(k):
        pl.semaphore_signal(barrier, 1, device_id=(sec, op_peer(k)), device_id_type=MESH)

    for other in (z * 2 + (core + 1) % 2, ((z + 1) % 8) * 2 + core, ((z + 7) % 8) * 2 + core):
        pl.semaphore_signal(barrier, 1, device_id=(other, op), device_id_type=MESH)

    def live(h, c):
        row = lax.broadcasted_iota(jnp.int32, (rows, width), 0) + op * rows
        column = lax.broadcasted_iota(jnp.int32, (rows, width), 1) + c * width
        return (row < counts[h]) & (column < counts[h])

    def gather_start(c):
        first, second = current[c, 0], current[c, 1]
        for j in range(blocks):
            chosen[c, j] = jnp.where(source[j] == 0, first, second)
        pltpu.make_async_copy(chosen.at[c, op], gathered.at[c, op], gather_recv.at[c]).start()

        @pl.loop(1, blocks)
        def _(k):
            peer = op_peer(k)
            pltpu.make_async_remote_copy(
                chosen.at[c, peer], gathered.at[c, op], gather_send.at[c], gather_recv.at[c],
                device_id=(sec, peer), device_id_type=MESH,
            ).start()

    def wait_for(ref, sem):
        pltpu.make_async_copy(ref, ref, sem).wait()

    for c in range(CHUNKS):
        for h in range(2):
            piece = theta[h, :, c * width : (c + 1) * width]
            current[c, h] = jnp.where(live(h, c), piece, 0.0)
    previous[...] = jnp.zeros_like(previous)
    running[blocks] = jnp.zeros((rows, width), F32)

    pl.semaphore_wait(barrier, blocks - 1 + 3)

    @pl.loop(0, CHUNKS)
    def _(c):
        gather_start(c)

    for b in range(blocks):
        found = jnp.int32(blocks)
        for a in range(b):
            found = jnp.where(target[a] == target[b], a, found)
        before[b] = found

    @pl.loop(0, sectors)
    def _(q):
        found = jnp.int32(blocks)
        for b in range(blocks):
            found = jnp.where(target[b] == q, b, found)
        final[q] = found

    load_left.wait()

    @pl.loop(0, pairs * size // 128)
    def _(i):
        p, r = i // (size // 128), pl.multiple_of((i % (size // 128)) * 128, 128)
        at = pl.multiple_of(i * 128, 128)
        high, low = split(left_raw[p, pl.ds(r, 128), :])
        left_hi[pl.ds(at, 128), :] = high
        left_lo[pl.ds(at, 128), :] = low

    load_right.wait()

    @pl.loop(0, CHUNKS)
    def _(c):
        for p in range(pairs):
            high, low = split(right_raw[p, pl.ds(pl.multiple_of(c * width, width), width), :])
            right_two[c, 0:width, p * size : (p + 1) * size] = high
            right_two[c, width : 2 * width, p * size : (p + 1) * size] = low

    def rows_start(c):
        pltpu.make_async_copy(terms.at[c, op], arrived.at[c, op], rows_recv.at[c]).start()

        @pl.loop(1, blocks)
        def _(k):
            peer = op_peer(k)
            pltpu.make_async_remote_copy(
                terms.at[c, peer], arrived.at[c, op], rows_send.at[c], rows_recv.at[c],
                device_id=(sec, peer), device_id_type=MESH,
            ).start()

    def ring_start(side, h, c, j, dest):
        near = ((z + 1 + 6 * side) % 8) * 2 + core
        pltpu.make_async_remote_copy(
            sums.at[c, dest], ring_in.at[h, side, j - 1, c], ring_send.at[c],
            ring_recv.at[h, side, j - 1, c],
            device_id=(near, op), device_id_type=MESH,
        ).start()

    def ring_dest(side, j):
        return (z + (5 - j) * (1 - side) + (3 + j) * side) % 8

    def ring_wait(side, h, j, c):
        wait_for(ring_in.at[h, side, j - 1, c], ring_recv.at[h, side, j - 1, c])

    def step(k):
        half = k % 2

        @pl.loop(0, CHUNKS)
        def _(c):
            wait_for(gathered.at[c], gather_recv.at[c])
            high, low = split(gathered[c].reshape(size, width))
            both = jnp.concatenate([high, low], axis=1)
            lane = pl.multiple_of(c * width, width)

            @pl.loop(0, pairs)
            def _(p):
                at = pl.multiple_of(p * size, size)
                a = jnp.dot(left_hi[pl.ds(at, size), :], both, preferred_element_type=F32)
                b = jnp.dot(left_lo[pl.ds(at, size), :], high, preferred_element_type=F32)
                x_high, x_low = split(a[:, :width] + a[:, width:] + b)
                x_hi[:, pl.ds(at + lane, width)] = x_high
                x_lo[:, pl.ds(at + lane, width)] = x_low

        @pl.loop(0, CHUNKS)
        def _(c):
            wait_for(gathered.at[c, 0 : blocks - 1], gather_send.at[c])

        @pl.loop(0, CHUNKS)
        def _(c):
            both, high = right_two[c], right_two[c, 0:width, :]
            for part in range(2):
                r = part * (size // 2)
                a = lax.dot_general(x_hi[r : r + size // 2, :], both, NT, preferred_element_type=F32)
                b = lax.dot_general(x_lo[r : r + size // 2, :], high, NT, preferred_element_type=F32)
                block_rows = a[:, :width] + a[:, width:] + b
                terms[c, part * (blocks // 2) : (part + 1) * (blocks // 2)] = block_rows.reshape(
                    blocks // 2, rows, width
                )
            rows_start(c)

        def sum_blocks(c):
            wait_for(arrived.at[c], rows_recv.at[c])
            for b in range(blocks):
                running[b] = arrived[c, b] + running[before[b]]
            for there in range(8):
                for h in range(2):
                    pass_out[c, there, h] = running[final[4 * there + 2 * (1 - core) + h]]
                    sums[c, there, h] = running[final[4 * there + 2 * core + h]]
            pltpu.make_async_remote_copy(
                pass_out.at[c], pass_in.at[half, c], pass_send.at[c], pass_recv.at[half, c],
                device_id=(z * 2 + (core + 1) % 2, op), device_id_type=MESH,
            ).start()

        def ring_first(c):
            wait_for(pass_in.at[half, c], pass_recv.at[half, c])
            sums[c] = sums[c] + pass_in[half, c]
            side = c % 2
            ring_start(side, half, c, 1, ring_dest(side, 1))

        def ring_second(c):
            side = c % 2
            other = 1 - side
            ring_start(other, half, c, 2, ring_dest(other, 2))
            ring_wait(side, half, 1, c)
            dest = ring_dest(side, 2)
            sums[c, dest] = sums[c, dest] + ring_in[half, side, 0, c]
            ring_start(side, half, c, 2, dest)

        def ring_next(c, j):
            for side in range(2):
                ring_wait(side, half, j - 1, c)
                dest = ring_dest(side, j)
                sums[c, dest] = sums[c, dest] + ring_in[half, side, j - 2, c]
                ring_start(side, half, c, j, dest)

        def finish(c):
            ring_wait(0, half, HOPS, c)
            ring_wait(1, half, HOPS, c)
            scale = jnp.where(k == 0, factor, 2.0 * factor).astype(F32)
            keep = jnp.where(k == 0, 0.0, 1.0).astype(F32)
            for h in range(2):
                total = sums[c, z, h] + ring_in[half, 0, HOPS - 1, c, h] + ring_in[half, 1, HOPS - 1, c, h]
                following = jnp.where(live(h, c), scale * total, 0.0) - keep * previous[c, h]
                previous[c, h] = current[c, h]
                current[c, h] = following

            @pl.when(k < STEPS - 1)
            def _():
                gather_start(c)

        stages = [
            sum_blocks, ring_first, ring_second,
            lambda c: ring_next(c, 3), lambda c: ring_next(c, 4), finish,
        ]

        @pl.loop(0, CHUNKS + len(stages) - 1)
        def _(t):
            for s in reversed(range(len(stages))):
                c = t - s

                @pl.when((c >= 0) & (c < CHUNKS))
                def _():
                    stages[s](c)

        @pl.loop(0, CHUNKS)
        def _(c):
            wait_for(arrived.at[c, 0 : blocks - 1], rows_send.at[c])
            wait_for(pass_out.at[c], pass_send.at[c])
            wait_for(sums.at[c, 0:7], ring_send.at[c])

    pl.loop(0, STEPS)(step)

    for c in range(CHUNKS):
        for h in range(2):
            last_out[h, :, c * width : (c + 1) * width] = current[c, h]
            prev_out[h, :, c * width : (c + 1) * width] = previous[c, h]


def per_device(theta, counts, pair_source, pair_target, left_ops, right_ops):
    sec_local, rows, size = theta.shape
    pairs = left_ops.shape[0]
    blocks = pair_target.shape[0]
    sectors = sec_local * lax.axis_size("sec")
    places = sectors // (2 * sec_local)
    factor = 0.5 / math.sqrt(blocks * pairs / sec_local)
    width = size // CHUNKS
    vmem, smem = pltpu.VMEM, pltpu.SMEM
    tile = (rows, width)
    flops = STEPS * pairs * 2 * 2 * 3 * size**3
    return pl.pallas_call(
        functools.partial(kernel, factor),
        out_shape=[jax.ShapeDtypeStruct(theta.shape, F32)] * 2,
        in_specs=[pl.BlockSpec(memory_space=vmem)]
        + [pl.BlockSpec(memory_space=smem)] * 3
        + [pl.BlockSpec(memory_space=pl.ANY)] * 2,
        out_specs=[pl.BlockSpec(memory_space=vmem)] * 2,
        scratch_shapes=[
            vmem(left_ops.shape, F32),
            vmem(left_ops.shape, F32),
            vmem((pairs * size, size), BF16),
            vmem((pairs * size, size), BF16),
            vmem((CHUNKS, 2 * width, pairs * size), BF16),
            vmem((size, pairs * size), BF16),
            vmem((size, pairs * size), BF16),
            vmem((CHUNKS, sec_local) + tile, F32),
            vmem((CHUNKS, sec_local) + tile, F32),
            vmem((CHUNKS, blocks) + tile, F32),
            vmem((CHUNKS, blocks) + tile, F32),
            vmem((CHUNKS, blocks) + tile, F32),
            vmem((CHUNKS, blocks) + tile, F32),
            vmem((blocks + 1,) + tile, F32),
            vmem((CHUNKS, places, sec_local) + tile, F32),
            vmem((2, CHUNKS, places, sec_local) + tile, F32),
            vmem((CHUNKS, places, sec_local) + tile, F32),
            vmem((2, 2, HOPS, CHUNKS, sec_local) + tile, F32),
            smem((blocks,), jnp.int32),
            smem((sectors,), jnp.int32),
            pltpu.SemaphoreType.DMA((2,)),
            pltpu.SemaphoreType.DMA((CHUNKS,)),
            pltpu.SemaphoreType.DMA((CHUNKS,)),
            pltpu.SemaphoreType.DMA((CHUNKS,)),
            pltpu.SemaphoreType.DMA((CHUNKS,)),
            pltpu.SemaphoreType.DMA((CHUNKS,)),
            pltpu.SemaphoreType.DMA((2, CHUNKS)),
            pltpu.SemaphoreType.DMA((CHUNKS,)),
            pltpu.SemaphoreType.DMA((2, 2, HOPS, CHUNKS)),
        ],
        compiler_params=pltpu.CompilerParams(
            collective_id=0, has_side_effects=True, vmem_limit_bytes=56 * 1024 * 1024
        ),
        cost_estimate=pl.CostEstimate(
            flops=flops, bytes_accessed=8 * left_ops.size, transcendentals=0
        ),
    )(theta, counts, pair_source, pair_target, left_ops, right_ops)


def solution(mesh):
    in_specs = (
        P("sec", "op", None),
        P("sec"),
        P("sec"),
        P("sec"),
        P(("sec", "op"), None, None),
        P(("sec", "op"), None, None),
    )
    out_specs = (P("sec", "op", None), P("sec", "op", None))
    return jax.shard_map(
        per_device, mesh=mesh, in_specs=in_specs, out_specs=out_specs, check_vma=False
    )
```

time: 680 us -> 150 us (0.22)
  waiting for transfers between devices: 496 us -> 0 us
  Pallas kernels: 0 us -> 144 us
  matrix products: 81 us -> 0 us
  blocking collectives: 58 us -> 0 us
  between operations: 16.7 us -> 0.64 us
  local copies, waits for them, and re-layouts: 14 us -> 3.14 us
  other arithmetic: 8.39 us -> 0 us
    psum x3 -> x0, waiting for transfers between devices: 345 us -> none  [hamiltonian(): whole_sums = lax.psum(sector_sums, 'sec')]
    all_gather x3 -> x0, waiting for transfers between devices: 151 us -> none  [hamiltonian(): gathered = lax.all_gather(iterate, 'op', axis=1, tiled=True)]
    pallas_call x0 -> x1, Pallas kernels: none -> 144 us  [per_device(): pl.pallas_call(functools.partial(kernel, factor), out_shape=[jax.ShapeDty...]
    dot_general x9 -> x0, matrix products: 81 us -> none  [the longest x3 41.5 us: hamiltonian(): jnp.einsum('pmk,pnk->mn', left_product, right_ops, precision=highest)]
    all_to_all x3 -> x0, blocking collectives: 58 us -> none  [hamiltonian(): lax.all_to_all(split_rows, 'op', split_axis=0, concat_axis=0, tiled=True)]
    dynamic_slice x7 -> x0, local copies, waits for them, and re-layouts: 12.6 us -> none  [the longest x6 11.4 us: hamiltonian(): chosen = lax.dynamic_index_in_dim(gathered, my_source, 0, keepdims=False)]
  transfers between devices with their start and end apart: 6 -> 0, of which waited for: 6 -> 0; matrix products, arithmetic and copies ran while one was open for 0% -> 0% of each run, Pallas kernels for 0% -> 0%
where the time goes in v1:
time: 150 us; the launch traced here: 148 us
  Pallas kernels  144 us (96%)
  local copies, waits for them, and re-layouts  3.14 us (2%)
    pallas_call x1, Pallas kernels, per_device(): pl.pallas_call(functools.partial(kernel, factor), out_shape=[jax.ShapeDty...  144 us
    unnamed x2, local copies, waits for them, and re-layouts  3.14 us

profile of v1, /device:TPU:1, one launch (start us, length us, event | category | flops | bytes accessed | tf_op | source)
XLA Modules:
  0.0 148.0 jit_solution(6175098565582791993)
XLA Ops:
  0.6 144.2 %shard_map.77 = (f32[2,32,512]{2,1,0:T(8,128)}, f32[2,32,512]{2,1,0:T(8,128)}) custom-call(f32[2,32,512]{2,1,0:T(8,128)} %theta.1, s32[2]{0:T(128)} %counts.1, s32[16]{0:T(128)} %source.1, s32[16]{0:T(128)} %target.1, f32[4,512,512]{2,1,0:T(8,128)} %left.1, f32[4,512,512]{2,1,0:T(8,128)} %right.1), custom_call_target="tpu_custom_call" | custom-call | flops 19327352832 | bytes 8388608 | tf_op jit(solution)/shard_map/pallas_call | solution.py:280
  144.8 1.6 %copy.10 = f32[2,32,512]{2,1,0:T(8,128)} copy(f32[2,32,512]{2,1,0:T(8,128)} %get-tuple-element.4) | data formatting | bytes 262144
  146.4 1.6 %copy.11 = f32[2,32,512]{2,1,0:T(8,128)} copy(f32[2,32,512]{2,1,0:T(8,128)} %get-tuple-element.5) | data formatting | bytes 262144

commit v2 on v1

v2 whole, which is shorter than its diff:
```python
import functools
import math

import jax
import jax.numpy as jnp
from jax import lax
from jax.experimental import pallas as pl
from jax.experimental.pallas import tpu as pltpu
from jax.sharding import PartitionSpec as P

STEPS = 3
CHUNKS = 4
CUTS = 2
PARTS = CHUNKS * CUTS
SLOTS = 4
PACE = 1
FIRST_AT, HUB_AT, FINISH_AT = 1, 4, 7
MESH = pl.DeviceIdType.MESH
F32 = jnp.float32
BF16 = jnp.bfloat16
NT = (((1,), (1,)), ((), ()))


def split(value):
    high = value.astype(BF16)
    return high, (value - high.astype(F32)).astype(BF16)


def kernel(
    factor,
    theta, counts, source, target, left, right,
    last_out, prev_out,
    left_raw, right_raw, left_hi, left_lo, right_two, x_hi, x_lo,
    current, previous, chosen, gathered, terms, arrived, running,
    pass_out, pass_in, sums, sums_in,
    before, final,
    load_sem, gather_send, gather_recv, rows_send, rows_recv,
    pass_send, pass_recv, sums_send, sums_recv,
):
    sec, op = lax.axis_index("sec"), lax.axis_index("op")
    z, core = sec // 2, sec % 2
    op_x, op_y = op // 4, op % 4
    size = left.shape[1]
    pairs = left.shape[0]
    width = size // CHUNKS
    rows = theta.shape[1]
    cut = rows // CUTS
    blocks = target.shape[0]
    sectors = final.shape[0]

    load_left = pltpu.make_async_copy(left, left_raw, load_sem.at[0])
    load_right = pltpu.make_async_copy(right, right_raw, load_sem.at[1])
    load_left.start()
    load_right.start()

    def op_peer(k):
        return ((op_x + k // 4) % 4) * 4 + (op_y + k % 4) % 4

    barrier = pltpu.get_barrier_semaphore()

    @pl.loop(1, blocks)
    def _(k):
        pl.semaphore_signal(barrier, 1, device_id=(sec, op_peer(k)), device_id_type=MESH)

    pl.semaphore_signal(barrier, 1, device_id=(z * 2 + (core + 1) % 2, op), device_id_type=MESH)
    for away in (1, 2, 6, 7):
        other = ((z + away) % 8) * 2 + core
        pl.semaphore_signal(barrier, 1, device_id=(other, op), device_id_type=MESH)

    def place(e):
        return e // CUTS, pl.ds(pl.multiple_of((e % CUTS) * cut, cut), cut)

    def live(h, e):
        row = lax.broadcasted_iota(jnp.int32, (cut, width), 0) + (op * rows + (e % CUTS) * cut)
        column = lax.broadcasted_iota(jnp.int32, (cut, width), 1) + (e // CUTS) * width
        return (row < counts[h]) & (column < counts[h])

    def gather_start(e):
        c, part = place(e)
        first, second = current[e, 0], current[e, 1]
        for j in range(blocks):
            chosen[e, j] = jnp.where(source[j] == 0, first, second)
        pltpu.make_async_copy(chosen.at[e, op], gathered.at[c, op, part], gather_recv.at[e]).start()

        @pl.loop(1, blocks)
        def _(k):
            peer = op_peer(k)
            pltpu.make_async_remote_copy(
                chosen.at[e, peer], gathered.at[c, op, part], gather_send.at[e], gather_recv.at[e],
                device_id=(sec, peer), device_id_type=MESH,
            ).start()

    def wait_for(ref, sem):
        pltpu.make_async_copy(ref, ref, sem).wait()

    for e in range(PARTS):
        c, r = e // CUTS, (e % CUTS) * cut
        for h in range(2):
            piece = theta[h, r : r + cut, c * width : (c + 1) * width]
            current[e, h] = jnp.where(live(h, e), piece, 0.0)
    previous[...] = jnp.zeros_like(previous)
    running[blocks] = jnp.zeros((cut, width), F32)

    pl.semaphore_wait(barrier, blocks - 1 + 5)

    @pl.loop(0, PARTS)
    def _(e):
        gather_start(e)

    for b in range(blocks):
        found = jnp.int32(blocks)
        for a in range(b):
            found = jnp.where(target[a] == target[b], a, found)
        before[b] = found

    @pl.loop(0, sectors)
    def _(q):
        found = jnp.int32(blocks)
        for b in range(blocks):
            found = jnp.where(target[b] == q, b, found)
        final[q] = found

    load_left.wait()

    @pl.loop(0, pairs * size // 128)
    def _(i):
        p, r = i // (size // 128), pl.multiple_of((i % (size // 128)) * 128, 128)
        at = pl.multiple_of(i * 128, 128)
        high, low = split(left_raw[p, pl.ds(r, 128), :])
        left_hi[pl.ds(at, 128), :] = high
        left_lo[pl.ds(at, 128), :] = low

    load_right.wait()

    @pl.loop(0, CHUNKS)
    def _(c):
        for p in range(pairs):
            high, low = split(right_raw[p, pl.ds(pl.multiple_of(c * width, width), width), :])
            right_two[c, 0:width, p * size : (p + 1) * size] = high
            right_two[c, width : 2 * width, p * size : (p + 1) * size] = low

    def rows_start(e):
        c, part = place(e)
        pltpu.make_async_copy(terms.at[c, op, part], arrived.at[e, op], rows_recv.at[e]).start()

        @pl.loop(1, blocks)
        def _(k):
            peer = op_peer(k)
            pltpu.make_async_remote_copy(
                terms.at[c, peer, part], arrived.at[e, op], rows_send.at[e], rows_recv.at[e],
                device_id=(sec, peer), device_id_type=MESH,
            ).start()

    def away(side, distance):
        return (z + distance + side * (8 - 2 * distance)) % 8

    def sums_start(side, h, e, slot, dest, distance):
        pltpu.make_async_remote_copy(
            sums.at[e, away(side, dest)], sums_in.at[h, side, slot, e], sums_send.at[e],
            sums_recv.at[h, side, slot, e],
            device_id=(away(side, distance) * 2 + core, op), device_id_type=MESH,
        ).start()

    def sums_wait(side, h, slot, e):
        wait_for(sums_in.at[h, side, slot, e], sums_recv.at[h, side, slot, e])

    def step(k):
        half = k % 2

        @pl.loop(0, CHUNKS)
        def _(c):
            for r in range(CUTS):
                e = c * CUTS + r
                wait_for(chosen.at[e], gather_recv.at[e])
            high, low = split(gathered[c].reshape(size, width))
            both = jnp.concatenate([high, low], axis=1)
            lane = pl.multiple_of(c * width, width)

            @pl.loop(0, pairs)
            def _(p):
                at = pl.multiple_of(p * size, size)
                a = jnp.dot(left_hi[pl.ds(at, size), :], both, preferred_element_type=F32)
                b = jnp.dot(left_lo[pl.ds(at, size), :], high, preferred_element_type=F32)
                x_high, x_low = split(a[:, :width] + a[:, width:] + b)
                x_hi[:, pl.ds(at + lane, width)] = x_high
                x_lo[:, pl.ds(at + lane, width)] = x_low

        @pl.loop(0, PARTS)
        def _(e):
            wait_for(chosen.at[e, 0 : blocks - 1], gather_send.at[e])

        @pl.loop(0, CHUNKS)
        def _(c):
            both, high = right_two[c], right_two[c, 0:width, :]
            for part in range(2):
                r = part * (size // 2)
                a = lax.dot_general(x_hi[r : r + size // 2, :], both, NT, preferred_element_type=F32)
                b = lax.dot_general(x_lo[r : r + size // 2, :], high, NT, preferred_element_type=F32)
                block_rows = a[:, :width] + a[:, width:] + b
                terms[c, part * (blocks // 2) : (part + 1) * (blocks // 2)] = block_rows.reshape(
                    blocks // 2, rows, width
                )
            for r in range(CUTS):
                rows_start(c * CUTS + r)

        def sum_blocks(e):
            wait_for(arrived.at[e], rows_recv.at[e])
            for b in range(blocks):
                running[b] = arrived[e, b] + running[before[b]]
            for there in range(8):
                for h in range(2):
                    pass_out[e, there, h] = running[final[4 * there + 2 * (1 - core) + h]]
            pltpu.make_async_remote_copy(
                pass_out.at[e], pass_in.at[half, e], pass_send.at[e], pass_recv.at[half, e],
                device_id=(z * 2 + (core + 1) % 2, op), device_id_type=MESH,
            ).start()
            for there in range(8):
                for h in range(2):
                    sums[e, there, h] = running[final[4 * there + 2 * core + h]]

        def sums_first(e):
            wait_for(pass_in.at[half, e], pass_recv.at[half, e])
            sums[e] = sums[e] + pass_in[half, e]
            sums_start(e % 2, half, e, 1, 4, 2)
            for side in range(2):
                sums_start(side, half, e, 0, 3, 1)
            for side in range(2):
                sums_start(side, half, e, 2, 1, 1)

        def sums_hub(e):
            for far in range(2):
                side = (e + 1 + far) % 2
                dest = away(side, 2)
                sums_wait(side, half, 0, e)
                total = sums[e, dest] + sums_in[half, side, 0, e]
                if far:
                    sums_wait(side, half, 1, e)
                    total = total + sums_in[half, side, 1, e]
                sums[e, dest] = total
                sums_start(side, half, e, 3, 2, 2)

        def finish(e):
            for side in range(2):
                sums_wait(side, half, 2, e)
                sums_wait(side, half, 3, e)
            scale = jnp.where(k == 0, factor, 2.0 * factor).astype(F32)
            keep = jnp.where(k == 0, 0.0, 1.0).astype(F32)
            for h in range(2):
                near = sums_in[half, 0, 2, e, h] + sums_in[half, 1, 2, e, h]
                far = sums_in[half, 0, 3, e, h] + sums_in[half, 1, 3, e, h]
                total = sums[e, z, h] + (near + far)
                following = jnp.where(live(h, e), scale * total, 0.0) - keep * previous[e, h]
                previous[e, h] = current[e, h]
                current[e, h] = following

            @pl.when(k < STEPS - 1)
            def _():
                gather_start(e)

        @pl.loop(0, (PARTS - 1) * PACE + FINISH_AT + 1)
        def _(t):
            def due(after, stage):
                wave = t - after
                e = wave // PACE

                @pl.when((wave >= 0) & (e < PARTS) & (wave % PACE == 0))
                def _():
                    stage(e)

            due(FINISH_AT, finish)
            due(HUB_AT, sums_hub)
            due(FIRST_AT, sums_first)
            due(0, sum_blocks)

        @pl.loop(0, PARTS)
        def _(e):
            wait_for(arrived.at[e, 0 : blocks - 1], rows_send.at[e])
            wait_for(pass_out.at[e], pass_send.at[e])
            wait_for(sums.at[e, 0:7], sums_send.at[e])

    pl.loop(0, STEPS)(step)

    for e in range(PARTS):
        c, r = e // CUTS, (e % CUTS) * cut
        for h in range(2):
            last_out[h, r : r + cut, c * width : (c + 1) * width] = current[e, h]
            prev_out[h, r : r + cut, c * width : (c + 1) * width] = previous[e, h]


def per_device(theta, counts, pair_source, pair_target, left_ops, right_ops):
    sec_local, rows, size = theta.shape
    pairs = left_ops.shape[0]
    blocks = pair_target.shape[0]
    sectors = sec_local * lax.axis_size("sec")
    places = sectors // (2 * sec_local)
    factor = 0.5 / math.sqrt(blocks * pairs / sec_local)
    width = size // CHUNKS
    vmem, smem = pltpu.VMEM, pltpu.SMEM
    tile = (rows // CUTS, width)
    flops = STEPS * pairs * 2 * 2 * 3 * size**3
    return pl.pallas_call(
        functools.partial(kernel, factor),
        out_shape=[jax.ShapeDtypeStruct(theta.shape, F32)] * 2,
        in_specs=[pl.BlockSpec(memory_space=vmem)]
        + [pl.BlockSpec(memory_space=smem)] * 3
        + [pl.BlockSpec(memory_space=pl.ANY)] * 2,
        out_specs=[pl.BlockSpec(memory_space=vmem)] * 2,
        scratch_shapes=[
            vmem(left_ops.shape, F32),
            vmem(left_ops.shape, F32),
            vmem((pairs * size, size), BF16),
            vmem((pairs * size, size), BF16),
            vmem((CHUNKS, 2 * width, pairs * size), BF16),
            vmem((size, pairs * size), BF16),
            vmem((size, pairs * size), BF16),
            vmem((PARTS, sec_local) + tile, F32),
            vmem((PARTS, sec_local) + tile, F32),
            vmem((PARTS, blocks) + tile, F32),
            vmem((CHUNKS, blocks, rows, width), F32),
            vmem((CHUNKS, blocks, rows, width), F32),
            vmem((PARTS, blocks) + tile, F32),
            vmem((blocks + 1,) + tile, F32),
            vmem((PARTS, places, sec_local) + tile, F32),
            vmem((2, PARTS, places, sec_local) + tile, F32),
            vmem((PARTS, places, sec_local) + tile, F32),
            vmem((2, 2, SLOTS, PARTS, sec_local) + tile, F32),
            smem((blocks,), jnp.int32),
            smem((sectors,), jnp.int32),
            pltpu.SemaphoreType.DMA((2,)),
            pltpu.SemaphoreType.DMA((PARTS,)),
            pltpu.SemaphoreType.DMA((PARTS,)),
            pltpu.SemaphoreType.DMA((PARTS,)),
            pltpu.SemaphoreType.DMA((PARTS,)),
            pltpu.SemaphoreType.DMA((PARTS,)),
            pltpu.SemaphoreType.DMA((2, PARTS)),
            pltpu.SemaphoreType.DMA((PARTS,)),
            pltpu.SemaphoreType.DMA((2, 2, SLOTS, PARTS)),
        ],
        compiler_params=pltpu.CompilerParams(
            collective_id=0, has_side_effects=True, vmem_limit_bytes=56 * 1024 * 1024
        ),
        cost_estimate=pl.CostEstimate(
            flops=flops, bytes_accessed=8 * left_ops.size, transcendentals=0
        ),
    )(theta, counts, pair_source, pair_target, left_ops, right_ops)


def solution(mesh):
    in_specs = (
        P("sec", "op", None),
        P("sec"),
        P("sec"),
        P("sec"),
        P(("sec", "op"), None, None),
        P(("sec", "op"), None, None),
    )
    out_specs = (P("sec", "op", None), P("sec", "op", None))
    return jax.shard_map(
        per_device, mesh=mesh, in_specs=in_specs, out_specs=out_specs, check_vma=False
    )
```

time: 150 us -> 132 us (0.88); the launches traced: 148 us -> 132 us
  Pallas kernels: 144 us -> 128 us
    pallas_call x1, Pallas kernels: 144 us -> 128 us  [per_device(): pl.pallas_call(functools.partial(kernel, factor), out_shape=[jax.ShapeDty...]
where the time goes in v2:
time: 132 us
  Pallas kernels  128 us (97%)
  local copies, waits for them, and re-layouts  3.14 us (2%)
    pallas_call x1, Pallas kernels, per_device(): pl.pallas_call(functools.partial(kernel, factor), out_shape=[jax.ShapeDty...  128 us
    unnamed x2, local copies, waits for them, and re-layouts  3.14 us

profile of v2, /device:TPU:1, one launch (start us, length us, event | category | flops | bytes accessed | tf_op | source)
XLA Modules:
  0.0 131.8 jit_solution(3009091838419015698)
XLA Ops:
  0.6 128.0 %shard_map.77 = (f32[2,32,512]{2,1,0:T(8,128)}, f32[2,32,512]{2,1,0:T(8,128)}) custom-call(f32[2,32,512]{2,1,0:T(8,128)} %theta.1, s32[2]{0:T(128)} %counts.1, s32[16]{0:T(128)} %source.1, s32[16]{0:T(128)} %target.1, f32[4,512,512]{2,1,0:T(8,128)} %left.1, f32[4,512,512]{2,1,0:T(8,128)} %right.1), custom_call_target="tpu_custom_call" | custom-call | flops 19327352832 | bytes 8388608 | tf_op jit(solution)/shard_map/pallas_call | solution.py:301
  128.6 1.6 %copy.10 = f32[2,32,512]{2,1,0:T(8,128)} copy(f32[2,32,512]{2,1,0:T(8,128)} %get-tuple-element.4) | data formatting | bytes 262144
  130.2 1.6 %copy.11 = f32[2,32,512]{2,1,0:T(8,128)} copy(f32[2,32,512]{2,1,0:T(8,128)} %get-tuple-element.5) | data formatting | bytes 262144

commit v3 on v2

--- a/solution.py
+++ b/solution.py
@@ -53,13 +53,17 @@
     load_left.start()
     load_right.start()
 
+    peer_x = [((op_x + k) % 4) * 4 for k in range(4)]
+    peer_y = [(op_y + k) % 4 for k in range(4)]
+
+    far_first = sorted(range(1, blocks), key=lambda k: -(min(k // 4, 4 - k // 4) + min(k % 4, 4 - k % 4)))
+
     def op_peer(k):
-        return ((op_x + k // 4) % 4) * 4 + (op_y + k % 4) % 4
+        return peer_x[k // 4] + peer_y[k % 4]
 
     barrier = pltpu.get_barrier_semaphore()
 
-    @pl.loop(1, blocks)
-    def _(k):
+    for k in range(1, blocks):
         pl.semaphore_signal(barrier, 1, device_id=(sec, op_peer(k)), device_id_type=MESH)
 
     pl.semaphore_signal(barrier, 1, device_id=(z * 2 + (core + 1) % 2, op), device_id_type=MESH)
@@ -82,8 +86,7 @@
             chosen[e, j] = jnp.where(source[j] == 0, first, second)
         pltpu.make_async_copy(chosen.at[e, op], gathered.at[c, op, part], gather_recv.at[e]).start()
 
-        @pl.loop(1, blocks)
-        def _(k):
+        for k in far_first:
             peer = op_peer(k)
             pltpu.make_async_remote_copy(
                 chosen.at[e, peer], gathered.at[c, op, part], gather_send.at[e], gather_recv.at[e],
@@ -136,15 +139,16 @@
     def _(c):
         for p in range(pairs):
             high, low = split(right_raw[p, pl.ds(pl.multiple_of(c * width, width), width), :])
-            right_two[c, 0:width, p * size : (p + 1) * size] = high
-            right_two[c, width : 2 * width, p * size : (p + 1) * size] = low
+            for d in range(CHUNKS):
+                at = (d * pairs + p) * width
+                right_two[c, 0:width, at : at + width] = high[:, d * width : (d + 1) * width]
+                right_two[c, width : 2 * width, at : at + width] = low[:, d * width : (d + 1) * width]
 
     def rows_start(e):
         c, part = place(e)
         pltpu.make_async_copy(terms.at[c, op, part], arrived.at[e, op], rows_recv.at[e]).start()
 
-        @pl.loop(1, blocks)
-        def _(k):
+        for k in far_first:
             peer = op_peer(k)
             pltpu.make_async_remote_copy(
                 terms.at[c, peer, part], arrived.at[e, op], rows_send.at[e], rows_recv.at[e],
@@ -167,14 +171,12 @@
     def step(k):
         half = k % 2
 
-        @pl.loop(0, CHUNKS)
-        def _(c):
+        def left_product(c):
             for r in range(CUTS):
                 e = c * CUTS + r
                 wait_for(chosen.at[e], gather_recv.at[e])
             high, low = split(gathered[c].reshape(size, width))
             both = jnp.concatenate([high, low], axis=1)
-            lane = pl.multiple_of(c * width, width)
 
             @pl.loop(0, pairs)
             def _(p):
@@ -182,24 +184,38 @@
                 a = jnp.dot(left_hi[pl.ds(at, size), :], both, preferred_element_type=F32)
                 b = jnp.dot(left_lo[pl.ds(at, size), :], high, preferred_element_type=F32)
                 x_high, x_low = split(a[:, :width] + a[:, width:] + b)
-                x_hi[:, pl.ds(at + lane, width)] = x_high
-                x_lo[:, pl.ds(at + lane, width)] = x_low
+                lane = pl.multiple_of((c * pairs + p) * width, width)
+                x_hi[:, pl.ds(lane, width)] = x_high
+                x_lo[:, pl.ds(lane, width)] = x_low
+
+        def right_product(c, first, last, add):
+            k_at = slice(first * pairs * width, last * pairs * width)
+            for part in range(2):
+                r = slice(part * (size // 2), (part + 1) * (size // 2))
+                to = slice(part * (blocks // 2), (part + 1) * (blocks // 2))
+                a = lax.dot_general(
+                    x_hi[r, k_at], right_two[c, :, k_at], NT, preferred_element_type=F32
+                )
+                b = lax.dot_general(
+                    x_lo[r, k_at], right_two[c, 0:width, k_at], NT, preferred_element_type=F32
+                )
+                block_rows = (a[:, :width] + a[:, width:] + b).reshape(blocks // 2, rows, width)
+                terms[c, to] = terms[c, to] + block_rows if add else block_rows
+
+        pl.loop(0, CHUNKS - 1)(left_product)
+        right_product(0, 0, CHUNKS - 1, False)
+        left_product(CHUNKS - 1)
+        right_product(0, CHUNKS - 1, CHUNKS, True)
+        for r in range(CUTS):
+            rows_start(r)
 
         @pl.loop(0, PARTS)
         def _(e):
             wait_for(chosen.at[e, 0 : blocks - 1], gather_send.at[e])
 
-        @pl.loop(0, CHUNKS)
+        @pl.loop(1, CHUNKS)
         def _(c):
-            both, high = right_two[c], right_two[c, 0:width, :]
-            for part in range(2):
-                r = part * (size // 2)
-                a = lax.dot_general(x_hi[r : r + size // 2, :], both, NT, preferred_element_type=F32)
-                b = lax.dot_general(x_lo[r : r + size // 2, :], high, NT, preferred_element_type=F32)
-                block_rows = a[:, :width] + a[:, width:] + b
-                terms[c, part * (blocks // 2) : (part + 1) * (blocks // 2)] = block_rows.reshape(
-                    blocks // 2, rows, width
-                )
+            right_product(c, 0, CHUNKS, False)
             for r in range(CUTS):
                 rows_start(c * CUTS + r)
 
@@ -287,6 +303,11 @@
             prev_out[h, r : r + cut, c * width : (c + 1) * width] = previous[e, h]
 
 
+def hand_over(last, prev, last_out, prev_out):
+    last_out[...] = last[...]
+    prev_out[...] = prev[...]
+
+
 def per_device(theta, counts, pair_source, pair_target, left_ops, right_ops):
     sec_local, rows, size = theta.shape
     pairs = left_ops.shape[0]
@@ -298,7 +319,7 @@
     vmem, smem = pltpu.VMEM, pltpu.SMEM
     tile = (rows // CUTS, width)
     flops = STEPS * pairs * 2 * 2 * 3 * size**3
-    return pl.pallas_call(
+    last, prev = pl.pallas_call(
         functools.partial(kernel, factor),
         out_shape=[jax.ShapeDtypeStruct(theta.shape, F32)] * 2,
         in_specs=[pl.BlockSpec(memory_space=vmem)]
@@ -343,6 +364,12 @@
             flops=flops, bytes_accessed=8 * left_ops.size, transcendentals=0
         ),
     )(theta, counts, pair_source, pair_target, left_ops, right_ops)
+    return pl.pallas_call(
+        hand_over,
+        out_shape=[jax.ShapeDtypeStruct(theta.shape, F32)] * 2,
+        in_specs=[pl.BlockSpec(memory_space=vmem)] * 2,
+        out_specs=[pl.BlockSpec(memory_space=vmem)] * 2,
+    )(last, prev)
 
 
 def solution(mesh):

time: 132 us -> 127 us (0.962)
  local copies, waits for them, and re-layouts: 3.14 us -> 0 us
  Pallas kernels: 128 us -> 126 us
    pallas_call x1, Pallas kernels: 128 us -> 125 us  [per_device(): pl.pallas_call(functools.partial(kernel, factor), out_shape=[jax.ShapeDty...]
    unnamed x2 -> x0, local copies, waits for them, and re-layouts: 3.14 us -> none
    pallas_call x0 -> x1, Pallas kernels: none -> 1.68 us  [per_device(): pl.pallas_call(hand_over, out_shape=[jax.ShapeDtypeStruct(theta.shape, F3...]
where the time goes in v3:
time: 127 us
  Pallas kernels  126 us (99%)
    pallas_call x1, Pallas kernels, per_device(): pl.pallas_call(functools.partial(kernel, factor), out_shape=[jax.ShapeDty...  125 us

profile of v3, /device:TPU:1, one launch (start us, length us, event | category | flops | bytes accessed | tf_op | source)
XLA Modules:
  0.0 127.1 jit_solution(13698379731324387142)
XLA Ops:
  0.6 124.8 %shard_map.77 = (f32[2,32,512]{2,1,0:T(8,128)}, f32[2,32,512]{2,1,0:T(8,128)}) custom-call(f32[2,32,512]{2,1,0:T(8,128)} %theta.1, s32[2]{0:T(128)} %counts.1, s32[16]{0:T(128)} %source.1, s32[16]{0:T(128)} %target.1, f32[4,512,512]{2,1,0:T(8,128)} %left.1, f32[4,512,512]{2,1,0:T(8,128)} %right.1), custom_call_target="tpu_custom_call" | custom-call | flops 19327352832 | bytes 8388608 | tf_op jit(solution)/shard_map/pallas_call | solution.py:322
  125.4 1.7 %shard_map.78 = (f32[2,32,512]{2,1,0:T(8,128)}, f32[2,32,512]{2,1,0:T(8,128)}) custom-call(f32[2,32,512]{2,1,0:T(8,128)} %get-tuple-element.4.last, f32[2,32,512]{2,1,0:T(8,128)} %get-tuple-element.5.prev), custom_call_target="tpu_custom_call" | custom-call | tf_op jit(solution)/shard_map/pallas_call | solution.py:367

commit v4 on v3

--- a/solution.py
+++ b/solution.py
@@ -178,9 +178,8 @@
             high, low = split(gathered[c].reshape(size, width))
             both = jnp.concatenate([high, low], axis=1)
 
-            @pl.loop(0, pairs)
-            def _(p):
-                at = pl.multiple_of(p * size, size)
+            for p in range(pairs):
+                at = p * size
                 a = jnp.dot(left_hi[pl.ds(at, size), :], both, preferred_element_type=F32)
                 b = jnp.dot(left_lo[pl.ds(at, size), :], high, preferred_element_type=F32)
                 x_high, x_low = split(a[:, :width] + a[:, width:] + b)

time: 127 us -> 122 us (0.961)
  Pallas kernels: 126 us -> 121 us
    pallas_call x1, Pallas kernels: 125 us -> 119 us  [per_device(): pl.pallas_call(functools.partial(kernel, factor), out_shape=[jax.ShapeDty...]
where the time goes in v4:
time: 122 us; the launch traced here: 121 us
  Pallas kernels  121 us (99%)
    pallas_call x1, Pallas kernels, per_device(): pl.pallas_call(functools.partial(kernel, factor), out_shape=[jax.ShapeDty...  119 us

profile of v4, /device:TPU:1, one launch (start us, length us, event | category | flops | bytes accessed | tf_op | source)
XLA Modules:
  0.0 121.3 jit_solution(16366246745341549181)
XLA Ops:
  0.6 119.0 %shard_map.77 = (f32[2,32,512]{2,1,0:T(8,128)}, f32[2,32,512]{2,1,0:T(8,128)}) custom-call(f32[2,32,512]{2,1,0:T(8,128)} %theta.1, s32[2]{0:T(128)} %counts.1, s32[16]{0:T(128)} %source.1, s32[16]{0:T(128)} %target.1, f32[4,512,512]{2,1,0:T(8,128)} %left.1, f32[4,512,512]{2,1,0:T(8,128)} %right.1), custom_call_target="tpu_custom_call" | custom-call | flops 19327352832 | bytes 8388608 | tf_op jit(solution)/shard_map/pallas_call | solution.py:321
  119.6 1.7 %shard_map.78 = (f32[2,32,512]{2,1,0:T(8,128)}, f32[2,32,512]{2,1,0:T(8,128)}) custom-call(f32[2,32,512]{2,1,0:T(8,128)} %get-tuple-element.4.last, f32[2,32,512]{2,1,0:T(8,128)} %get-tuple-element.5.prev), custom_call_target="tpu_custom_call" | custom-call | tf_op jit(solution)/shard_map/pallas_call | solution.py:366

commit v5 on v4

--- a/solution.py
+++ b/solution.py
@@ -212,8 +212,7 @@
         def _(e):
             wait_for(chosen.at[e, 0 : blocks - 1], gather_send.at[e])
 
-        @pl.loop(1, CHUNKS)
-        def _(c):
+        for c in range(1, CHUNKS):
             right_product(c, 0, CHUNKS, False)
             for r in range(CUTS):
                 rows_start(c * CUTS + r)

time: 122 us -> 122 us (level)
  no operation moved by 1% of the time
where the time goes in v5:
time: 122 us; the launch traced here: 121 us
  Pallas kernels  121 us (99%)
    pallas_call x1, Pallas kernels, per_device(): pl.pallas_call(functools.partial(kernel, factor), out_shape=[jax.ShapeDty...  119 us

profile of v5, /device:TPU:1, one launch (start us, length us, event | category | flops | bytes accessed | tf_op | source)
XLA Modules:
  0.0 121.2 jit_solution(7015716030184381120)
XLA Ops:
  0.6 118.9 %shard_map.77 = (f32[2,32,512]{2,1,0:T(8,128)}, f32[2,32,512]{2,1,0:T(8,128)}) custom-call(f32[2,32,512]{2,1,0:T(8,128)} %theta.1, s32[2]{0:T(128)} %counts.1, s32[16]{0:T(128)} %source.1, s32[16]{0:T(128)} %target.1, f32[4,512,512]{2,1,0:T(8,128)} %left.1, f32[4,512,512]{2,1,0:T(8,128)} %right.1), custom_call_target="tpu_custom_call" | custom-call | flops 19327352832 | bytes 8388608 | tf_op jit(solution)/shard_map/pallas_call | solution.py:320
  119.5 1.7 %shard_map.78 = (f32[2,32,512]{2,1,0:T(8,128)}, f32[2,32,512]{2,1,0:T(8,128)}) custom-call(f32[2,32,512]{2,1,0:T(8,128)} %get-tuple-element.4.last, f32[2,32,512]{2,1,0:T(8,128)} %get-tuple-element.5.prev), custom_call_target="tpu_custom_call" | custom-call | tf_op jit(solution)/shard_map/pallas_call | solution.py:365
